TPU v7x, 256 devices: a whole 4x4x8 slice. The times are simulated.
256 devices in a mesh: grp: 8 (over y_lo, x), seq: 32 (over z, y_hi, core).
Axes of the slice: x: 4, y: 4 (y_hi: 2, y_lo: 2; y = y_hi * 2 + y_lo), z: 8, core: 2. Of those that a mesh axis runs over, the one named last changes fastest.
Arguments:
- fake_tokens: bfloat16 [8, 6144, 1536], P('grp', 'seq'), may hold values from -16 to 16
- real_tokens: bfloat16 [8, 6144, 1536], P('grp', 'seq'), may hold values from -6 to 6
- proj_weight: bfloat16 [1536, 2048], P('seq'), may hold values from -0.15625 to 0.15625
- score_vector: float32 [2048], replicated, may hold values from -0.25 to 0.25
Outputs:
- grad_weight: float32 [1536, 2048], P('seq')
All inputs are finite; a program needn't handle non-finite values.
Results may differ from a plain program's by a relative error of at most 0.0003.
Values may be sent and summed in bfloat16 or wider, within the bound.
No kernel may reach another device: no remote copies, remote signals or barrier semaphores. Data moves between devices by JAX's collectives and lax.ppermute only.
A program may use at most 64 MiB of HBM per device.

v0:
```python
import math
import jax
import jax.numpy as jnp
from jax import lax
from jax.sharding import PartitionSpec as P

R1_WEIGHT = 40.0


def per_device(fake_tokens, real_tokens, proj_weight, score_vector):
    fake_rows = fake_tokens[0]
    real_rows = real_tokens[0]
    tok_count = fake_rows.shape[0]
    hid_width = proj_weight.shape[1]
    loss_scale = math.sqrt(hid_width / (lax.axis_size("grp") * lax.axis_size("seq") * tok_count))
    joined = jnp.concatenate([fake_rows, real_rows], 0)
    shard_rows = lax.all_gather(proj_weight, "seq", axis=0, tiled=True)
    partial_pre = jnp.dot(joined, shard_rows, preferred_element_type=jnp.float32)
    full_weight = shard_rows
    preact, full_weight = (partial_pre, full_weight)
    squash = jax.nn.sigmoid(preact)
    slopes = squash * (1.0 + preact * (1.0 - squash))
    curves = squash * (1.0 - squash) * (2.0 + preact * (1.0 - 2.0 * squash))
    logits = jnp.dot(preact * squash, score_vector, precision=lax.Precision.HIGHEST)
    slopes_real = slopes[tok_count:]
    lifted = (slopes_real * score_vector).astype(jnp.bfloat16)
    input_grad = lax.dot_general(
        lifted, full_weight, (((1,), (1,)), ((), ())), preferred_element_type=jnp.float32
    )
    r1_cot = (loss_scale * R1_WEIGHT * input_grad).astype(jnp.bfloat16)
    back_grad = jnp.dot(r1_cot, full_weight, preferred_element_type=jnp.float32)
    fake_cot = (
        loss_scale * jax.nn.sigmoid(logits[:tok_count])[:, None] * slopes[:tok_count] * score_vector
    ).astype(jnp.bfloat16)
    real_cot = (
        -loss_scale * jax.nn.sigmoid(-logits[tok_count:])[:, None] * slopes_real * score_vector
        + back_grad * score_vector * curves[tok_count:]
    ).astype(jnp.bfloat16)
    left_rows = jnp.concatenate([fake_rows, real_rows, r1_cot], 0)
    right_rows = jnp.concatenate([fake_cot, real_cot, lifted], 0)
    grad_term = lax.dot_general(
        left_rows, right_rows, (((0,), (0,)), ((), ())), preferred_element_type=jnp.float32
    )
    grad_shard = lax.psum_scatter(grad_term, "seq", scatter_dimension=0, tiled=True)
    return lax.psum(grad_shard, "grp")


def solution(mesh):
    in_specs = (P("grp", "seq", None), P("grp", "seq", None), P("seq", None), P())
    out_specs = P("seq", None)
    return jax.shard_map(
        per_device, mesh=mesh, in_specs=in_specs, out_specs=out_specs, check_vma=False
    )
```

profile of v0, /device:TPU:32, one launch (start us, length us, event | category | flops | bytes accessed | tf_op | source)
XLA Modules:
  0.0 387.8 jit_solution(6854587875983400413)
XLA Ops:
  6.5 0.0 all-gather.2.cloned.1.call-start
  6.5 0.7 all-gather.2.cloned.1.call-update
  7.3 0.0 reduce-scatter.2.cloned.1.call-start
  7.3 99.7 %all-gather.2.cloned.1.call-done = bf16[1536,2048]{1,0:T(8,128)(2,1)} async-done(((bf16[48,2048]{1,0:T(8,128)(2,1)}), bf16[1536,2048]{1,0:T(8,128)(2,1)}) %all-gather.2.cloned.1.call-update) | async-done | bytes 6291472 | tf_op jit(solution)/shard_map/all_gather | solution.py:17
  107.0 0.0 copy-start
  107.0 5.6 %add_divide_fusion = (f32[384,2048]{1,0:T(8,128)S(1)}, f32[384,2048]{1,0:T(8,128)S(1)}, f32[384,2048]{1,0:T(8,128)S(1)}, f32[384,2048]{1,0:T(8,128)S(1)}) fusion(bf16[1536,2048]{1,0:T(8,128)(2,1)} %all-gather.2.cloned.1.call-done, bf16[192,1536]{1,0:T(8,128)(2,1)} %bitcast.12, bf16[192,1536]{1,0:T(8,128)(2,1)} %bitcast.14), kind=kOutput, calls=%fused_computation.3 | convolution fusion | flops 2423783424 | bytes 20054016 | tf_op jit(solution)/shard_map/dot_general | solution.py:18
  112.6 0.0 slice-start
  112.6 0.0 copy-done
  112.6 0.0 slice-start.1
  112.6 3.3 fusion.25
  115.9 0.1 divide_multiply_fusion.1
  116.0 0.3 fusion.20
  116.3 0.0 slice-done
  116.3 0.0 slice-done.1
  116.3 2.2 fusion.5
  118.6 0.0 copy-start.1
  118.6 0.0 copy-start.2
  118.6 1.8 fusion.4
  120.4 0.0 copy-done.1
  120.4 0.0 copy-done.2
  120.4 8.0 %fusion.6 = f32[1536,2048]{1,0:T(8,128)} fusion(bf16[192,2048]{1,0:T(8,128)(2,1)S(1)} %get-tuple-element.6, bf16[192,2048]{1,0:T(8,128)(2,1)S(1)} %fusion.4, bf16[192,2048]{1,0:T(8,128)(2,1)S(1)} %get-tuple-element.5, bf16[192,1536]{1,0:T(8,128)(2,1)S(1)} %fusion.5, bf16[192,1536]{1,0:T(8,128)(2,1)S(1)} %bitcast.13, bf16[192,1536]{1,0:T(8,128)(2,1)S(1)} %bitcast.15), kind=kOutput, calls=%fused_computation.10 | convolution fusion | flops 3636264960 | bytes 16711680 | tf_op jit(solution)/shard_map/dot_general | solution.py:41
  128.4 0.0 reduce-scatter.2.cloned.1.call-update
  128.5 0.0 all-reduce.2.cloned.1.call-start
  128.5 169.6 %reduce-scatter.2.cloned.1.call-done = f32[48,2048]{1,0:T(8,128)} async-done(((f32[1536,2048]{1,0:T(8,128)}), f32[48,2048]{1,0:T(8,128)}) %reduce-scatter.2.cloned.1.call-update) | async-done | bytes 393232 | tf_op jit(solution)/shard_map/reduce_scatter | solution.py:44
  298.1 0.0 all-reduce.2.cloned.1.call-update
  298.1 81.3 %all-reduce.2.cloned.1.call-done = f32[48,2048]{1,0:T(8,128)} async-done(((f32[48,2048]{1,0:T(8,128)}), f32[48,2048]{1,0:T(8,128)}) %all-reduce.2.cloned.1.call-update) | async-done | bytes 393232 | tf_op jit(solution)/shard_map/psum | solution.py:45
  379.5 1.8 copy.6
  (1 shorter events, 0.0 us)
Async XLA Ops:
  6.5 100.4 %all-gather.2.cloned.1.call-start = ((), (), s32[]{:S(2)}) async-start(), calls=%async_computation.1 | async-start | bytes 6488064 | tf_op jit(solution)/shard_map/all_gather | solution.py:17
  7.3 290.9 %reduce-scatter.2.cloned.1.call-start = ((), (), s32[]{:S(2)}) async-start(), calls=%async_computation.2 | async-start | bytes 12976128 | tf_op jit(solution)/shard_map/reduce_scatter | solution.py:44
  107.0 5.6 %copy-start = (f32[2048]{0:T(1024)S(1)}, f32[2048]{0:T(1024)}, u32[]{:S(2)}) copy-start(f32[2048]{0:T(1024)} %param.7) | copy-start | bytes 24580
  112.6 3.7 slice-start
  112.6 3.7 slice-start.1
  118.6 1.9 copy-start.1
  118.6 1.9 copy-start.2
  128.5 251.0 %all-reduce.2.cloned.1.call-start = ((), (), s32[]{:S(2)}) async-start(), calls=%async_computation.3 | async-start | bytes 786432 | tf_op jit(solution)/shard_map/psum | solution.py:45
Sparse Core Ops, SparseCore 0:
  10.1 96.7 all-gather.1
  128.6 169.4 reduce-scatter.1
  300.7 78.6 all-reduce.1
where the time goes:
time: 388 us
  waiting for transfers between devices  351 us (90%)
  matrix products  20.9 us (5%)
  between operations  13.2 us (3%)
    reduce_scatter x1, waiting for transfers between devices, per_device(): lax.psum_scatter(grad_term, 'seq', scatter_dimension=0, tiled=True)  170 us
    all_gather x1, waiting for transfers between devices, per_device(): shard_rows = lax.all_gather(proj_weight, 'seq', axis=0, tiled=True)  99.7 us
    psum x1, waiting for transfers between devices, per_device(): return lax.psum(grad_shard, 'grp')  81.3 us
    dot_general x1, matrix products, per_device(): lax.dot_general(left_rows, right_rows, (((0,), (0,)), ((), ())), preferre...  8.01 us
  transfers between devices with their start and end apart: 3, of which 3 were waited for; matrix products, arithmetic and copies ran while one was open for 0% of the time, Pallas kernels for 0%

commit v1 on v0

--- a/solution.py
+++ b/solution.py
@@ -42,7 +42,7 @@
         left_rows, right_rows, (((0,), (0,)), ((), ())), preferred_element_type=jnp.float32
     )
     grad_shard = lax.psum_scatter(grad_term, "seq", scatter_dimension=0, tiled=True)
-    return lax.psum(grad_shard, "grp")
+    return jnp.sum(lax.all_gather(grad_shard, "grp"), axis=0)
 
 
 def solution(mesh):

time: 388 us -> 355 us (0.915)
  waiting for transfers between devices: 351 us -> 318 us
    psum x1 -> x0, waiting for transfers between devices: 81.3 us -> none  [per_device(): return lax.psum(grad_shard, 'grp')]
    all_gather x0 -> x1, waiting for transfers between devices: none -> 47.6 us  [per_device(): return jnp.sum(lax.all_gather(grad_shard, 'grp'), axis=0)]
where the time goes in v1:
time: 355 us
  waiting for transfers between devices  318 us (90%)
  matrix products  20.9 us (6%)
  between operations  13.2 us (4%)
    reduce_scatter x1, waiting for transfers between devices, per_device(): lax.psum_scatter(grad_term, 'seq', scatter_dimension=0, tiled=True)  170 us
    all_gather x1, waiting for transfers between devices, per_device(): shard_rows = lax.all_gather(proj_weight, 'seq', axis=0, tiled=True)  99.7 us
    all_gather x1, waiting for transfers between devices, per_device(): return jnp.sum(lax.all_gather(grad_shard, 'grp'), axis=0)  47.6 us
    dot_general x1, matrix products, per_device(): lax.dot_general(left_rows, right_rows, (((0,), (0,)), ((), ())), preferre...  8.01 us
  transfers between devices with their start and end apart: 3, of which 3 were waited for; matrix products, arithmetic and copies ran while one was open for 0% of the time, Pallas kernels for 0%

profile of v1, /device:TPU:32, one launch (start us, length us, event | category | flops | bytes accessed | tf_op | source)
XLA Modules:
  0.0 355.1 jit_solution(12180093741783458351)
XLA Ops:
  6.5 0.0 all-gather.4.cloned.1.call-start
  6.5 0.7 all-gather.4.cloned.1.call-update
  7.3 0.0 reduce-scatter.2.cloned.1.call-start
  7.3 99.7 %all-gather.4.cloned.1.call-done = bf16[1536,2048]{1,0:T(8,128)(2,1)} async-done(((bf16[48,2048]{1,0:T(8,128)(2,1)}), bf16[1536,2048]{1,0:T(8,128)(2,1)}) %all-gather.4.cloned.1.call-update) | async-done | bytes 6291472 | tf_op jit(solution)/shard_map/all_gather | solution.py:17
  107.0 0.0 copy-start
  107.0 5.6 %add_divide_fusion = (f32[384,2048]{1,0:T(8,128)S(1)}, f32[384,2048]{1,0:T(8,128)S(1)}, f32[384,2048]{1,0:T(8,128)S(1)}, f32[384,2048]{1,0:T(8,128)S(1)}) fusion(bf16[1536,2048]{1,0:T(8,128)(2,1)} %all-gather.4.cloned.1.call-done, bf16[192,1536]{1,0:T(8,128)(2,1)} %bitcast.14, bf16[192,1536]{1,0:T(8,128)(2,1)} %bitcast.16), kind=kOutput, calls=%fused_computation.3 | convolution fusion | flops 2423783424 | bytes 20054016 | tf_op jit(solution)/shard_map/dot_general | solution.py:18
  112.6 0.0 slice-start
  112.6 0.0 copy-done
  112.6 0.0 slice-start.1
  112.6 3.3 fusion.25
  115.9 0.1 divide_multiply_fusion.1
  116.0 0.3 fusion.20
  116.3 0.0 slice-done
  116.3 0.0 slice-done.1
  116.3 2.2 fusion.5
  118.6 0.0 copy-start.1
  118.6 0.0 copy-start.2
  118.6 1.8 fusion.4
  120.4 0.0 copy-done.1
  120.4 0.0 copy-done.2
  120.4 8.0 %fusion.6 = f32[1536,2048]{1,0:T(8,128)} fusion(bf16[192,2048]{1,0:T(8,128)(2,1)S(1)} %get-tuple-element.6, bf16[192,2048]{1,0:T(8,128)(2,1)S(1)} %fusion.4, bf16[192,2048]{1,0:T(8,128)(2,1)S(1)} %get-tuple-element.5, bf16[192,1536]{1,0:T(8,128)(2,1)S(1)} %fusion.5, bf16[192,1536]{1,0:T(8,128)(2,1)S(1)} %bitcast.15, bf16[192,1536]{1,0:T(8,128)(2,1)S(1)} %bitcast.17), kind=kOutput, calls=%fused_computation.10 | convolution fusion | flops 3636264960 | bytes 16711680 | tf_op jit(solution)/shard_map/dot_general | solution.py:41
  128.4 0.0 reduce-scatter.2.cloned.1.call-update
  128.5 0.0 all-gather.6.cloned.1.call-start
  128.5 169.6 %reduce-scatter.2.cloned.1.call-done = f32[48,2048]{1,0:T(8,128)} async-done(((f32[1536,2048]{1,0:T(8,128)}), f32[48,2048]{1,0:T(8,128)}) %reduce-scatter.2.cloned.1.call-update) | async-done | bytes 393232 | tf_op jit(solution)/shard_map/reduce_scatter | solution.py:44
  298.1 0.0 all-gather.6.cloned.1.call-update
  298.1 47.6 %all-gather.6.cloned.1.call-done = f32[384,2048]{1,0:T(8,128)} async-done(((f32[48,2048]{1,0:T(8,128)}), f32[384,2048]{1,0:T(8,128)}) %all-gather.6.cloned.1.call-update) | async-done | bytes 3145744 | tf_op jit(solution)/shard_map/all_gather | solution.py:45
  345.8 2.8 reduce_sum.9
  (1 shorter events, 0.0 us)
Async XLA Ops:
  6.5 100.4 %all-gather.4.cloned.1.call-start = ((), (), s32[]{:S(2)}) async-start(), calls=%async_computation.1 | async-start | bytes 6488064 | tf_op jit(solution)/shard_map/all_gather | solution.py:17
  7.3 290.9 %reduce-scatter.2.cloned.1.call-start = ((), (), s32[]{:S(2)}) async-start(), calls=%async_computation.2 | async-start | bytes 12976128 | tf_op jit(solution)/shard_map/reduce_scatter | solution.py:44
  107.0 5.6 %copy-start = (f32[2048]{0:T(1024)S(1)}, f32[2048]{0:T(1024)}, u32[]{:S(2)}) copy-start(f32[2048]{0:T(1024)} %param.7) | copy-start | bytes 24580
  112.6 3.7 %slice-start = ((s8[6291456]{0:T(1024)(128)(4,1)}), s8[4194304]{0:T(1024)(128)(4,1)S(1)}, s32[]{:S(2)}) async-start(s8[6291456]{0:T(1024)(128)(4,1)} %bitcast.12), calls=%async_computation.4 | async-start | bytes 8388608
  112.6 3.7 %slice-start.1 = ((s8[6291456]{0:T(1024)(128)(4,1)}), s8[2097152]{0:T(1024)(128)(4,1)S(1)}, s32[]{:S(2)}) async-start(s8[6291456]{0:T(1024)(128)(4,1)} %bitcast.12), calls=%async_computation.5 | async-start | bytes 4194304
  118.6 1.9 copy-start.1
  118.6 1.9 copy-start.2
  128.5 217.3 %all-gather.6.cloned.1.call-start = ((), (), s32[]{:S(2)}) async-start(), calls=%async_computation.3 | async-start | bytes 3538944 | tf_op jit(solution)/shard_map/all_gather | solution.py:45
Sparse Core Ops, SparseCore 0:
  10.1 96.7 all-gather.3
  128.6 169.4 reduce-scatter.1
  299.9 45.8 all-gather.5

commit v2 on v0

--- a/solution.py
+++ b/solution.py
@@ -14,7 +14,9 @@
     hid_width = proj_weight.shape[1]
     loss_scale = math.sqrt(hid_width / (lax.axis_size("grp") * lax.axis_size("seq") * tok_count))
     joined = jnp.concatenate([fake_rows, real_rows], 0)
-    shard_rows = lax.all_gather(proj_weight, "seq", axis=0, tiled=True)
+    shard_rows = jnp.concatenate(
+        lax.all_to_all(jnp.stack([proj_weight] * lax.axis_size("seq")), "seq", 0, 0), axis=0
+    )
     partial_pre = jnp.dot(joined, shard_rows, preferred_element_type=jnp.float32)
     full_weight = shard_rows
     preact, full_weight = (partial_pre, full_weight)

time: 388 us -> 439 us (1.13)
  blocking collectives: 0 us -> 152 us
  waiting for transfers between devices: 351 us -> 251 us
    all_to_all x0 -> x1, blocking collectives: none -> 152 us  [per_device(): lax.all_to_all(jnp.stack([proj_weight] * lax.axis_size('seq')), 'seq', 0, 0)]
    all_gather x1 -> x0, waiting for transfers between devices: 99.7 us -> none  [per_device(): shard_rows = lax.all_gather(proj_weight, 'seq', axis=0, tiled=True)]
  transfers between devices with their start and end apart: 3 -> 2, of which waited for: 3 -> 2; matrix products, arithmetic and copies ran while one was open for 0% -> 0% of each run, Pallas kernels for 0% -> 0%
where the time goes in v2:
time: 439 us
  waiting for transfers between devices  251 us (57%)
  blocking collectives  152 us (35%)
  matrix products  18.7 us (4%)
  between operations  13.5 us (3%)
    reduce_scatter x1, waiting for transfers between devices, per_device(): lax.psum_scatter(grad_term, 'seq', scatter_dimension=0, tiled=True)  170 us
    all_to_all x1, blocking collectives, per_device(): lax.all_to_all(jnp.stack([proj_weight] * lax.axis_size('seq')), 'seq', 0, 0)  152 us
    psum x1, waiting for transfers between devices, per_device(): return lax.psum(grad_shard, 'grp')  81.2 us
  transfers between devices with their start and end apart: 2, of which 2 were waited for; matrix products, arithmetic and copies ran while one was open for 0% of the time, Pallas kernels for 0%

profile of v2, /device:TPU:32, one launch (start us, length us, event | category | flops | bytes accessed | tf_op | source)
XLA Modules:
  0.0 439.1 jit_solution(9125207531550973211)
XLA Ops:
  6.5 0.0 reduce-scatter.2.cloned.1.call-start
  6.5 1.7 stack.2
  8.3 0.0 copy-start.1
  8.3 0.0 copy-start.2
  8.3 151.7 %all_to_all.5 = bf16[32,48,2048]{2,1,0:T(8,128)(2,1)S(1)} all-to-all(bf16[32,48,2048]{2,1,0:T(8,128)(2,1)S(1)} %stack.2), channel_id=1, replica_groups=mesh['grp'=8,'seq'=32] {'seq'}, dimensions={0} | all-to-all | bytes 12582912 | tf_op jit(solution)/shard_map/all_to_all | solution.py:18
  160.0 0.0 copy-done.1
  160.0 0.0 copy-done.2
  160.0 0.0 copy-start
  160.0 3.1 add_divide_fusion
  163.1 0.0 copy-done
  163.1 3.3 fusion.25
  166.4 0.1 divide_multiply_fusion.1
  166.5 0.3 fusion.20
  166.8 2.3 fusion.5
  169.1 1.9 fusion.4
  171.0 8.1 %fusion.6 = f32[1536,2048]{1,0:T(8,128)} fusion(bf16[192,2048]{1,0:T(8,128)(2,1)S(1)} %get-tuple-element.6, bf16[192,2048]{1,0:T(8,128)(2,1)S(1)} %fusion.4, bf16[192,2048]{1,0:T(8,128)(2,1)S(1)} %get-tuple-element.5, bf16[192,1536]{1,0:T(8,128)(2,1)S(1)} %fusion.5, bf16[192,1536]{1,0:T(8,128)(2,1)S(1)} %bitcast.15, bf16[192,1536]{1,0:T(8,128)(2,1)S(1)} %bitcast.17), kind=kOutput, calls=%fused_computation.10 | convolution fusion | flops 3636264960 | bytes 16711680 | tf_op jit(solution)/shard_map/dot_general | solution.py:43
  179.1 0.0 reduce-scatter.2.cloned.1.call-update
  179.1 0.0 all-reduce.2.cloned.1.call-start
  179.2 170.1 %reduce-scatter.2.cloned.1.call-done = f32[48,2048]{1,0:T(8,128)} async-done(((f32[1536,2048]{1,0:T(8,128)}), f32[48,2048]{1,0:T(8,128)}) %reduce-scatter.2.cloned.1.call-update) | async-done | bytes 393232 | tf_op jit(solution)/shard_map/reduce_scatter | solution.py:46
  349.2 0.0 all-reduce.2.cloned.1.call-update
  349.3 81.2 %all-reduce.2.cloned.1.call-done = f32[48,2048]{1,0:T(8,128)} async-done(((f32[48,2048]{1,0:T(8,128)}), f32[48,2048]{1,0:T(8,128)}) %all-reduce.2.cloned.1.call-update) | async-done | bytes 393232 | tf_op jit(solution)/shard_map/psum | solution.py:47
  430.5 1.8 copy.6
Async XLA Ops:
  6.5 342.7 %reduce-scatter.2.cloned.1.call-start = ((), (), s32[]{:S(2)}) async-start(), calls=%async_computation.2 | async-start | bytes 12976128 | tf_op jit(solution)/shard_map/reduce_scatter | solution.py:46
  8.3 151.7 %copy-start.1 = (bf16[1,192,1536]{2,1,0:T(8,128)(2,1)S(1)}, bf16[1,192,1536]{2,1,0:T(8,128)(2,1)}, u32[]{:S(2)}) copy-start(bf16[1,192,1536]{2,1,0:T(8,128)(2,1)} %param.5) | copy-start | bytes 1769476
  8.3 151.7 %copy-start.2 = (bf16[1,192,1536]{2,1,0:T(8,128)(2,1)S(1)}, bf16[1,192,1536]{2,1,0:T(8,128)(2,1)}, u32[]{:S(2)}) copy-start(bf16[1,192,1536]{2,1,0:T(8,128)(2,1)} %param.4) | copy-start | bytes 1769476
  160.0 3.1 copy-start
  179.1 251.4 %all-reduce.2.cloned.1.call-start = ((), (), s32[]{:S(2)}) async-start(), calls=%async_computation.3 | async-start | bytes 786432 | tf_op jit(solution)/shard_map/psum | solution.py:47
Sparse Core Ops, SparseCore 0:
  179.3 169.9 reduce-scatter.1
  351.9 78.6 all-reduce.1
